TPU v7x, 32 devices: a whole 2x2x4 slice. The times are simulated.
32 devices in a mesh: grp: 2 (over x), patch: 4 (over y, core), wring: 4 (over z).
Axes of the slice: x: 2, y: 2, z: 4, core: 2. Of those that a mesh axis runs over, the one named last changes fastest.
Arguments:
- tokens: bfloat16 [4096, 6144], P(('grp', 'patch', 'wring')), parts along dimension 0, may hold values from -6 to 6
- mod_scale: float32 [6144], replicated, may hold values from -1.5 to 1.5
- mod_shift: float32 [6144], replicated, may hold values from -1.5 to 1.5
- q_weight: bfloat16 [6144, 3072], P(None, 'wring'), may hold values from -0.078125 to 0.078125
- q_gain: float32 [3072], P('wring'), may hold values from 1.5 to 3
- stale_keys: bfloat16 [4096, 3072], P(('grp', 'patch'), 'wring'), parts along dimension 0, may hold values from -6 to 6
- stale_values: bfloat16 [4096, 3072], P(('grp', 'patch'), 'wring'), parts along dimension 0, may hold values from -12 to 12
- kv_lists: int32 [8, 4, 1], P('grp'), parts along dimension 0, may hold values from -1 to 3, as said below
- block_mask: int32 [32, 16], P('grp'), parts along dimension 0, may hold values from 0 to 1, as said below
Outputs:
- attended: bfloat16 [4096, 3072], P(('grp', 'patch'), 'wring'), parts along dimension 0
There are 2 independent parts, one for each index of `grp`. A program takes and returns all parts, laid end to end along the dimension named above; an argument that names none is the same for every part. Nothing has to cross between parts.
Inputs may be any that keep to these rules, and one draw needn't show every extreme that they name: kv_lists[d, s, j] holds distinct block numbers within patch s in its first slots and -1 after them; all slots are -1 when d == s; each pair lists at most 1 block, and in every draw one patch reads 1 block from every other patch. block_mask[a, a] is 1; block_mask[a, b] is 1 for a block b of another patch only where b is listed for the two patches in kv_lists; every listed block is attended by some query block of the reading patch.
All inputs are finite; a program needn't handle non-finite values.
Results may differ from a plain program's by a relative error of at most 0.012.
Values may be sent and summed in bfloat16 or wider, within the bound.
A program may use at most 128 MiB of HBM per device.

v0:
```python
import math

import jax
import jax.numpy as jnp
from jax import lax
from jax.sharding import PartitionSpec as P

DH = 128
BLK = 128


def rms_rows(values):
    return values * lax.rsqrt(jnp.mean(values * values, axis=-1, keepdims=True) + 1e-06)


def on_device(
    tokens, mod_scale, mod_shift, q_weight, q_gain, stale_keys, stale_values, kv_lists, block_mask
):
    floats = tokens.astype(jnp.float32)
    centre = jnp.mean(floats, axis=-1, keepdims=True)
    spread = jnp.mean((floats - centre) * (floats - centre), axis=-1, keepdims=True)
    normed = ((floats - centre) * lax.rsqrt(spread + 1e-06) * (1.0 + mod_scale) + mod_shift).astype(
        jnp.bfloat16
    )
    queries = jnp.dot(
        lax.all_gather(normed, "wring", axis=0, tiled=True),
        q_weight,
        preferred_element_type=jnp.float32,
    ).astype(jnp.bfloat16)
    patch_rows = queries.shape[0]
    columns = queries.shape[1]
    heads_here = columns // DH
    q_hat = rms_rows(
        queries.astype(jnp.float32).reshape(patch_rows, heads_here, DH)
    ) * q_gain.reshape(heads_here, DH)
    q_hat = q_hat.astype(jnp.bfloat16).reshape(patch_rows, columns)
    k_hat = (
        rms_rows(stale_keys.astype(jnp.float32).reshape(patch_rows, heads_here, DH))
        .astype(jnp.bfloat16)
        .reshape(patch_rows, columns)
    )
    blocks_here = patch_rows // BLK
    patches = lax.axis_size("patch")
    my_patch = lax.axis_index("patch")
    incoming = lax.dynamic_index_in_dim(kv_lists, my_patch, 0, keepdims=False)
    remote = (
        jnp.arange(patches, dtype=jnp.int32)[:, None] * blocks_here + jnp.maximum(incoming, 0)
    ).reshape(-1)
    outgoing = lax.dynamic_index_in_dim(kv_lists, my_patch, 1, keepdims=False)
    slot_count = outgoing.shape[1]
    chosen = jnp.maximum(outgoing, 0)
    sending = (outgoing >= 0)[:, :, None, None]
    nothing = jnp.zeros((), jnp.bfloat16)
    send_keys = jnp.where(sending, k_hat.reshape(blocks_here, BLK, columns)[chosen], nothing)
    send_values = jnp.where(
        sending, stale_values.reshape(blocks_here, BLK, columns)[chosen], nothing
    )
    send_keys = send_keys.reshape(patches, slot_count * BLK, columns)
    send_values = send_values.reshape(patches, slot_count * BLK, columns)
    got_keys, got_values = (
        lax.all_to_all(send_keys, "patch", split_axis=0, concat_axis=0, tiled=True),
        lax.all_to_all(send_values, "patch", split_axis=0, concat_axis=0, tiled=True),
    )
    got_keys = got_keys.reshape(-1, columns)
    got_values = got_values.reshape(-1, columns)
    block_ids = jnp.concatenate(
        [my_patch * blocks_here + jnp.arange(blocks_here, dtype=jnp.int32), remote]
    )
    usable = jnp.concatenate(
        [jnp.ones((blocks_here,), jnp.float32), (incoming >= 0).reshape(-1).astype(jnp.float32)]
    )
    mask_rows = lax.dynamic_slice_in_dim(block_mask, my_patch * blocks_here, blocks_here, 0).astype(
        jnp.float32
    )
    lookup = (
        block_ids[None, :] == jnp.arange(block_mask.shape[1], dtype=jnp.int32)[:, None]
    ).astype(jnp.float32)
    allowed = (
        jnp.dot(
            mask_rows, lookup, precision=lax.Precision.HIGHEST, preferred_element_type=jnp.float32
        )
        * usable[None, :]
    )
    all_keys = jnp.concatenate([k_hat, got_keys], axis=0)
    all_values = jnp.concatenate([stale_values, got_values], axis=0)
    key_blocks = block_ids.shape[0]
    row_step = min(512, patch_rows)
    step_blocks = row_step // BLK
    inverse_root = 1.0 / math.sqrt(DH)
    head_outputs = []
    for head_index in range(heads_here):
        head_keys = all_keys[:, head_index * DH : (head_index + 1) * DH]
        head_values = all_values[:, head_index * DH : (head_index + 1) * DH]
        pieces = []
        for row_start in range(0, patch_rows, row_step):
            query_head = q_hat[
                row_start : row_start + row_step, head_index * DH : (head_index + 1) * DH
            ]
            scores = jnp.einsum(
                "qd,kd->qk", query_head, head_keys, preferred_element_type=jnp.float32
            )
            block_start = row_start // BLK
            weights = jnp.exp(scores * inverse_root).reshape(step_blocks, BLK, key_blocks, BLK)
            weights = weights * allowed[block_start : block_start + step_blocks, None, :, None]
            weights = weights.reshape(row_step, key_blocks * BLK)
            shares = (weights / jnp.sum(weights, axis=1, keepdims=True)).astype(jnp.bfloat16)
            pieces.append(
                jnp.dot(shares, head_values, preferred_element_type=jnp.float32).astype(
                    jnp.bfloat16
                )
            )
        head_outputs.append(jnp.concatenate(pieces, axis=0))
    return jnp.concatenate(head_outputs, axis=1)


def solution(mesh):
    placed = (
        P(("grp", "patch", "wring"), None),
        P(),
        P(),
        P(None, "wring"),
        P("wring"),
        P(("grp", "patch"), "wring"),
        P(("grp", "patch"), "wring"),
        P("grp", None, None),
        P("grp", None),
    )
    return jax.shard_map(
        on_device,
        mesh=mesh,
        in_specs=placed,
        out_specs=P(("grp", "patch"), "wring"),
        check_vma=False,
    )
```

profile of v0, /device:TPU:0, one launch (start us, length us, event | category | flops | bytes accessed | tf_op | source)
XLA Modules:
  0.0 178.7 jit_solution(7346488116907666296)
XLA Ops:
  7.4 1.7 convert_reduce_fusion
  9.7 1.8 %fusion.5 = bf16[128,6144]{1,0:T(8,128)(2,1)} fusion(bf16[128,6144]{1,0:T(8,128)(2,1)S(1)} %copy-done, f32[6144]{0:T(1024)S(1)} %copy-done.9, f32[6144]{0:T(1024)S(1)} %broadcast_add_fusion, f32[128]{0:T(128)S(1)} %add_rsqrt_fusion.2, f32[128]{0:T(128)S(1)} %broadcast_multiply_fusion), kind=kLoop, calls=%fused_computation.9 | loop fusion | flops 4718592 | bytes 3195904 | tf_op jit(solution)/shard_map/convert_element_type | solution.py:22
  15.1 1.8 mul.166
  16.9 1.7 copy.20
  18.9 1.9 %gather_fusion.1 = bf16[4,128,768]{2,1,0:T(8,128)(2,1)S(1)} fusion(bf16[4,128,768]{2,1,0:T(8,128)(2,1)} %bitcast.39, s32[1024]{0:T(1024)S(1)} %pad_clamp_fusion), kind=kCustom, calls=%fused_computation.1 | custom fusion | bytes 1572880 | tf_op jit(solution)/shard_map/gather | solution.py:56
  20.7 2.6 %multiply_convert_fusion = bf16[4,128,768]{2,1,0:T(8,128)(2,1)} fusion(f32[4,128,768]{2,1,0:T(8,128)S(1)} %bitcast.37, f32[4,128,768]{2,1,0:T(8,128)} %copy.20), kind=kLoop, calls=%fused_computation.48 | loop fusion | flops 786432 | bytes 3932160 | tf_op jit(solution)/shard_map/convert_element_type | solution.py:39
  23.3 1.8 %gather_fusion = bf16[4,128,768]{2,1,0:T(8,128)(2,1)S(1)} fusion(bf16[4,128,768]{2,1,0:T(8,128)(2,1)} %multiply_convert_fusion, s32[1024]{0:T(1024)S(1)} %pad_clamp_fusion), kind=kCustom, calls=%fused_computation | custom fusion | bytes 1572880 | tf_op jit(solution)/shard_map/gather | solution.py:54
  26.8 4.5 %all-to-all-start = ((bf16[4,128,768]{2,1,0:T(8,128)(2,1)}), bf16[4,128,768]{2,1,0:T(8,128)(2,1)S(1)}, u32[]{:S(2)}, u32[]{:S(2)}) async-start(bf16[4,128,768]{2,1,0:T(8,128)(2,1)} %get-tuple-element.6), calls=%async_computation | async-start | bytes 1572864 | tf_op jit(solution)/shard_map/all_to_all | solution.py:61
  32.4 10.5 %all-to-all-done = bf16[4,128,768]{2,1,0:T(8,128)(2,1)S(1)} async-done(((bf16[4,128,768]{2,1,0:T(8,128)(2,1)}), bf16[4,128,768]{2,1,0:T(8,128)(2,1)S(1)}, u32[]{:S(2)}, u32[]{:S(2)}) %all-to-all-start) | async-done | bytes 786464 | tf_op jit(solution)/shard_map/all_to_all | solution.py:61
  42.9 4.4 %all-to-all-start.1 = ((bf16[4,128,768]{2,1,0:T(8,128)(2,1)}), bf16[4,128,768]{2,1,0:T(8,128)(2,1)}, u32[]{:S(2)}, u32[]{:S(2)}) async-start(bf16[4,128,768]{2,1,0:T(8,128)(2,1)} %get-tuple-element.5), calls=%async_computation.1 | async-start | bytes 1572864 | tf_op jit(solution)/shard_map/all_to_all | solution.py:62
  47.6 82.2 %all-gather.2.cloned.1.call-done = bf16[512,6144]{1,0:T(8,128)(2,1)} async-done(((bf16[128,6144]{1,0:T(8,128)(2,1)}), bf16[512,6144]{1,0:T(8,128)(2,1)}) %all-gather.2.cloned.1.call-update) | async-done | bytes 6291472 | tf_op jit(solution)/shard_map/all_gather | solution.py:26
  129.8 10.9 %convert_multiply_fusion.1 = (f32[512,768]{1,0:T(8,128)}, bf16[512,768]{1,0:T(8,128)(2,1)}) fusion(bf16[512,6144]{1,0:T(8,128)(2,1)} %all-gather.2.cloned.1.call-done, bf16[6144,768]{1,0:T(8,128)(2,1)} %param.12), kind=kOutput, calls=%fused_computation.43 | convolution fusion | flops 4833017856 | bytes 18087936 | tf_op jit(solution)/shard_map/dot_general | solution.py:25
  140.6 1.9 %copy.16 = f32[512,768]{0,1:T(8,128)S(1)} copy(f32[512,768]{1,0:T(8,128)} %get-tuple-element.7) | data formatting | bytes 3145728 | tf_op jit(solution)/shard_map/mul | solution.py:13
  144.1 1.9 %copy.17 = f32[512,768]{1,0:T(8,128)S(1)} copy(f32[512,768]{0,1:T(8,128)} %bitcast.35) | data formatting | bytes 3145728 | tf_op jit(solution)/shard_map/mul | solution.py:13
  147.5 2.1 %fusion.59 = (f32[512]{0:T(512)S(1)}, f32[512,1024]{1,0:T(8,128)}) fusion(f32[64,8,8,128]{3,2,1,0:T(8,128)S(1)} %bitcast.28, bf16[512,768]{0,1:T(8,128)(2,1)S(1)} %fusion.8, bf16[512,768]{0,1:T(8,128)(2,1)S(1)} %copy.21, bf16[512,768]{1,0:T(8,128)(2,1)S(1)} %fusion.7), kind=kOutput, calls=%fused_computation.117 | convolution fusion | flops 136314368 | bytes 5900288 | tf_op jit(solution)/shard_map/qd,kd->qk/dot_general | solution.py:99
  149.6 2.1 %fusion.60 = (f32[512]{0:T(512)S(1)}, f32[512,1024]{1,0:T(8,128)}) fusion(f32[64,8,8,128]{3,2,1,0:T(8,128)S(1)} %bitcast.29, bf16[512,768]{0,1:T(8,128)(2,1)S(1)} %fusion.8, bf16[512,768]{0,1:T(8,128)(2,1)S(1)} %copy.21, bf16[512,768]{1,0:T(8,128)(2,1)S(1)} %fusion.7), kind=kOutput, calls=%fused_computation.118 | convolution fusion | flops 136314368 | bytes 5900288 | tf_op jit(solution)/shard_map/qd,kd->qk/dot_general | solution.py:99
  151.7 2.1 %fusion.61 = (f32[512]{0:T(512)S(1)}, f32[512,1024]{1,0:T(8,128)}) fusion(f32[64,8,8,128]{3,2,1,0:T(8,128)S(1)} %bitcast.30, bf16[512,768]{0,1:T(8,128)(2,1)S(1)} %fusion.8, bf16[512,768]{0,1:T(8,128)(2,1)S(1)} %copy.21, bf16[512,768]{1,0:T(8,128)(2,1)S(1)} %fusion.7), kind=kOutput, calls=%fused_computation.119 | convolution fusion | flops 136314368 | bytes 5900288 | tf_op jit(solution)/shard_map/qd,kd->qk/dot_general | solution.py:99
  153.8 2.1 %fusion.62 = (f32[512]{0:T(512)S(1)}, f32[512,1024]{1,0:T(8,128)}) fusion(f32[64,8,8,128]{3,2,1,0:T(8,128)S(1)} %bitcast.31, bf16[512,768]{0,1:T(8,128)(2,1)S(1)} %fusion.8, bf16[512,768]{0,1:T(8,128)(2,1)S(1)} %copy.21, bf16[512,768]{1,0:T(8,128)(2,1)S(1)} %fusion.7), kind=kOutput, calls=%fused_computation.120 | convolution fusion | flops 136314368 | bytes 5900288 | tf_op jit(solution)/shard_map/qd,kd->qk/dot_general | solution.py:99
  156.0 2.2 %fusion.63 = (f32[512]{0:T(512)S(1)}, f32[512,1024]{1,0:T(8,128)}) fusion(f32[64,8,8,128]{3,2,1,0:T(8,128)S(1)} %bitcast.32, bf16[512,768]{0,1:T(8,128)(2,1)S(1)} %fusion.8, bf16[512,768]{0,1:T(8,128)(2,1)S(1)} %copy.21, bf16[512,768]{1,0:T(8,128)(2,1)S(1)} %fusion.7), kind=kOutput, calls=%fused_computation.121 | convolution fusion | flops 136314368 | bytes 5900288 | tf_op jit(solution)/shard_map/qd,kd->qk/dot_general | solution.py:99
  158.1 2.1 %fusion.64 = (f32[512]{0:T(512)S(1)}, f32[512,1024]{1,0:T(8,128)}) fusion(f32[64,8,8,128]{3,2,1,0:T(8,128)S(1)} %bitcast.33, bf16[512,768]{0,1:T(8,128)(2,1)S(1)} %copy.21, bf16[512,768]{0,1:T(8,128)(2,1)S(1)} %fusion.8, bf16[512,768]{1,0:T(8,128)(2,1)S(1)} %fusion.7), kind=kOutput, calls=%fused_computation.122 | convolution fusion | flops 136314368 | bytes 5900288 | tf_op jit(solution)/shard_map/qd,kd->qk/dot_general | solution.py:99
  160.2 2.3 %fusion.14 = bf16[512,768]{0,1:T(8,128)(2,1)S(1)} fusion(f32[512,1024]{1,0:T(8,128)} %get-tuple-element.10, f32[512]{0:T(512)S(1)} %get-tuple-element.9, bf16[512,768]{1,0:T(8,128)(2,1)S(1)} %copy-done.8, bf16[512,768]{1,0:T(8,128)(2,1)} %bitcast.9), kind=kOutput, calls=%fused_computation.61 | convolution fusion | flops 135856128 | bytes 3803136 | tf_op jit(solution)/shard_map/dot_general | solution.py:108
  162.6 1.6 fusion.13
  164.2 1.6 fusion.12
  167.5 1.6 fusion.10
  (57 shorter events, 15.7 us)
Async XLA Ops:
  6.5 2.6 %copy-start = (bf16[128,6144]{1,0:T(8,128)(2,1)S(1)}, bf16[128,6144]{1,0:T(8,128)(2,1)}, u32[]{:S(2)}) copy-start(bf16[128,6144]{1,0:T(8,128)(2,1)} %param.9) | copy-start | bytes 4718596
  6.5 3.2 %copy-start.9 = (f32[6144]{0:T(1024)S(1)}, f32[6144]{0:T(1024)}, u32[]{:S(2)}) copy-start(f32[6144]{0:T(1024)} %param.11) | copy-start | bytes 73732
  6.5 123.2 %all-gather.2.cloned.1.call-start = ((), (), s32[]{:S(2)}) async-start(), calls=%async_computation.2 | async-start | bytes 7864320 | tf_op jit(solution)/shard_map/all_gather | solution.py:26
  9.7 1.9 %copy-start.7 = (bf16[512,768]{1,0:T(8,128)(2,1)S(1)}, bf16[512,768]{1,0:T(8,128)(2,1)}, u32[]{:S(2)}) copy-start(bf16[512,768]{1,0:T(8,128)(2,1)} %param.14) | copy-start | bytes 2359300
  16.9 1.7 copy-start.10
  18.6 2.1 %copy-start.1 = (f32[512,768]{1,0:T(8,128)S(1)}, f32[512,768]{1,0:T(8,128)}, u32[]{:S(2)}) copy-start(f32[512,768]{1,0:T(8,128)} %copy.19) | copy-start | bytes 4718596
  26.8 16.1 %all-to-all-start = ((bf16[4,128,768]{2,1,0:T(8,128)(2,1)}), bf16[4,128,768]{2,1,0:T(8,128)(2,1)S(1)}, u32[]{:S(2)}, u32[]{:S(2)}) async-start(bf16[4,128,768]{2,1,0:T(8,128)(2,1)} %get-tuple-element.6), calls=%async_computation | async-start | bytes 1572864 | tf_op jit(solution)/shard_map/all_to_all | solution.py:61
  42.9 117.3 %all-to-all-start.1 = ((bf16[4,128,768]{2,1,0:T(8,128)(2,1)}), bf16[4,128,768]{2,1,0:T(8,128)(2,1)}, u32[]{:S(2)}, u32[]{:S(2)}) async-start(bf16[4,128,768]{2,1,0:T(8,128)(2,1)} %get-tuple-element.5), calls=%async_computation.1 | async-start | bytes 1572864 | tf_op jit(solution)/shard_map/all_to_all | solution.py:62
  142.7 3.2 %copy-start.11 = (f32[768]{0:T(1024)S(1)}, f32[768]{0:T(1024)}, u32[]{:S(2)}) copy-start(f32[768]{0:T(1024)} %param.13) | copy-start | bytes 9220
  158.1 2.1 %copy-start.8 = (bf16[512,768]{1,0:T(8,128)(2,1)S(1)}, bf16[512,768]{1,0:T(8,128)(2,1)}, u32[]{:S(2)}) copy-start(bf16[512,768]{1,0:T(8,128)(2,1)} %param.15) | copy-start | bytes 2359300
  160.2 2.3 %copy-start.6 = (f32[512,1024]{1,0:T(8,128)S(1)}, f32[512,1024]{1,0:T(8,128)}, u32[]{:S(2)}) copy-start(f32[512,1024]{1,0:T(8,128)} %get-tuple-element.12) | copy-start | bytes 6291460
  162.5 1.7 copy-start.5
  164.2 1.7 copy-start.4
  165.9 1.7 copy-start.3
  167.5 1.7 copy-start.2
Sparse Core Ops, SparseCore 0:
  11.7 118.0 all-gather.1
where the time goes:
time: 179 us
  waiting for transfers between devices  92.7 us (52%)
  matrix products  34.6 us (19%)
  local copies, waits for them, and re-layouts  17.2 us (10%)
  between operations  13.7 us (8%)
  other arithmetic  11.6 us (6%)
  starting transfers between devices  8.86 us (5%)
    all_gather x1, waiting for transfers between devices, on_device(): lax.all_gather(normed, 'wring', axis=0, tiled=True)  82.2 us
    dot_general x6, matrix products, on_device(): jnp.einsum('qd,kd->qk', query_head, head_keys, preferred_element_type=jnp...  12.7 us
    dot_general x1, matrix products, on_device(): jnp.dot(lax.all_gather(normed, 'wring', axis=0, tiled=True), q_weight, pr...  10.9 us
    all_to_all x1, waiting for transfers between devices, on_device(): lax.all_to_all(send_keys, 'patch', split_axis=0, concat_axis=0, tiled=True)  10.5 us
    dot_general x6, matrix products, on_device(): jnp.dot(shares, head_values, preferred_element_type=jnp.float32)  10.2 us
    mul x5, local copies, waits for them, and re-layouts, rms_rows(): values * lax.rsqrt(jnp.mean(values * values, axis=-1, keepdims=True) + 1e...  8.04 us
    all_to_all x1, starting transfers between devices, on_device(): lax.all_to_all(send_keys, 'patch', split_axis=0, concat_axis=0, tiled=True)  4.47 us
    all_to_all x1, starting transfers between devices, on_device(): lax.all_to_all(send_values, 'patch', split_axis=0, concat_axis=0, tiled=T...  4.39 us
  transfers between devices with their start and end apart: 3, of which 2 were waited for; matrix products, arithmetic and copies ran while one was open for 26% of the time, Pallas kernels for 0%

commit v1 on v0

v1 whole, which is shorter than its diff:
```python
import functools
import math

import jax
import jax.numpy as jnp
from jax import lax
from jax.experimental import pallas as pl
from jax.experimental.pallas import tpu as pltpu
from jax.sharding import PartitionSpec as P

DH = 128
BLK = 128
CHUNKS = 8
F32 = jnp.float32
BF16 = jnp.bfloat16
SCORE_SCALE = math.log2(math.e) / math.sqrt(DH)


def rms_rows(values):
    return values * lax.rsqrt(jnp.mean(values * values, axis=-1, keepdims=True) + 1e-06)


def body(
    n, patches, slots,
    tok, scale, shift, w_hbm, gain, k_hbm, v_hbm, lists, mask, out,
    held, w, acc, qh, kraw, vall, khat, sendkv,
    w_sem, kv_sem, send_sem, recv_sem, kvs_sem, kvr_sem,
):
    me = lax.axis_index("wring")
    mp = lax.axis_index("patch")
    rows = tok.shape[0]
    width = tok.shape[1]
    kc = width // CHUNKS
    heads = gain.shape[1] // DH
    local = k_hbm.shape[0]
    bp = local // BLK

    w_copy = pltpu.make_async_copy(w_hbm, w, w_sem)
    w_copy.start()
    k_copy = pltpu.make_async_copy(k_hbm, kraw.at[pl.ds(0, local)], kv_sem.at[0])
    v_copy = pltpu.make_async_copy(v_hbm, vall.at[pl.ds(0, local)], kv_sem.at[1])
    k_copy.start()
    v_copy.start()

    barrier = pltpu.get_barrier_semaphore()

    @pl.when(me > 0)
    def _():
        pl.semaphore_signal(barrier, inc=1, device_id={"wring": me - 1})

    @pl.when(me < n - 1)
    def _():
        pl.semaphore_signal(barrier, inc=1, device_id={"wring": me + 1})

    for o in range(1, patches):
        pl.semaphore_signal(barrier, inc=1, device_id={"patch": lax.rem(mp + o, patches)})

    step = 16

    def norm_rows(i, carry):
        at = pl.ds(pl.multiple_of(i * step, step), step)
        x = tok[at, :].astype(F32)
        centred = x - jnp.mean(x, axis=-1, keepdims=True)
        spread = jnp.mean(centred * centred, axis=-1, keepdims=True)
        y = centred * lax.rsqrt(spread + 1e-06) * (1.0 + scale[...]) + shift[...]
        y = y.astype(BF16)
        for c in range(CHUNKS):
            held[me, c, at, :] = y[:, c * kc : (c + 1) * kc]
        return carry

    lax.fori_loop(0, rows // step, norm_rows, 0)

    edges = jnp.where(me > 0, 1, 0) + jnp.where(me < n - 1, 1, 0)
    pl.semaphore_wait(barrier, edges + patches - 1)

    def hop(shard, c, way):
        return pltpu.make_async_remote_copy(
            src_ref=held.at[shard, c],
            dst_ref=held.at[shard, c],
            send_sem=send_sem.at[way, shard, c],
            recv_sem=recv_sem.at[shard, c],
            device_id={"wring": me - 1 if way == 0 else me + 1},
        )

    def each(fn):
        def one(c, carry):
            fn(c)
            return carry

        lax.fori_loop(0, CHUNKS, one, 0)

    def send_own(c):
        @pl.when(me > 0)
        def _():
            hop(me, c, 0).start()

        @pl.when(me < n - 1)
        def _():
            hop(me, c, 1).start()

    each(send_own)

    k_copy.wait()
    v_copy.wait()

    def kv_copy(o, j, which):
        slot = (o - 1) * slots + j
        return pltpu.make_async_remote_copy(
            src_ref=sendkv.at[slot, which],
            dst_ref=(kraw, vall)[which].at[pl.ds(local + slot * BLK, BLK)],
            send_sem=kvs_sem.at[slot, which],
            recv_sem=kvr_sem.at[slot, which],
            device_id={"patch": lax.rem(mp + o, patches)},
        )

    pairs = [(o, j) for o in range(1, patches) for j in range(slots)]
    for o, j in pairs:
        slot = (o - 1) * slots + j
        picked = jnp.maximum(lists[lax.rem(mp + o, patches), mp, j], 0)
        for which, blocks in enumerate((kraw, vall)):
            chosen = jnp.zeros((BLK, sendkv.shape[3]), F32)
            for b in range(bp):
                chosen = chosen + blocks[b * BLK : (b + 1) * BLK, :].astype(F32) * (
                    jnp.where(picked == b, 1, 0).astype(F32)
                )
            sendkv[slot, which] = chosen.astype(BF16)
        kv_copy(o, j, 0).start()
        kv_copy(o, j, 1).start()

    w_copy.wait()

    def project(shard, c, way):
        part = jnp.dot(
            held[shard, c],
            w[pl.ds(pl.multiple_of(c * kc, kc), kc), :],
            preferred_element_type=F32,
        )

        @pl.when(c == 0)
        def _():
            acc[way] = part

        @pl.when(c > 0)
        def _():
            acc[way] = acc[way] + part

    each(lambda c: project(me, c, 0))

    for o, j in pairs:
        for which in range(2):
            kv_copy(o, j, which).wait_recv()
            kv_copy(o, j, which).wait_send()

    def norm_keys(i, carry):
        at = pl.ds(pl.multiple_of(i * BLK, BLK), BLK)
        for h in range(heads):
            lanes = slice(h * DH, (h + 1) * DH)
            khat[at, lanes] = rms_rows(kraw[at, lanes].astype(F32)).astype(BF16)
        return carry

    lax.fori_loop(0, khat.shape[0] // BLK, norm_keys, 0)

    def attend(shard, way):
        for h in range(heads):
            lanes = slice(h * DH, (h + 1) * DH)
            q = acc[way, :, lanes].astype(BF16).astype(F32)
            qh[:, lanes] = (rms_rows(q) * gain[:, lanes]).astype(BF16)
        for a in range(rows // BLK):
            row = mp * bp + shard * (rows // BLK) + a
            flags = [mask[row, mp * bp + b] for b in range(bp)]
            for o, j in pairs:
                owner = lax.rem(mp + patches - o, patches)
                listed = lists[mp, owner, j]
                flag = 0
                for b in range(bp):
                    flag = flag + jnp.where(listed == b, mask[row, owner * bp + b], 0)
                flags.append(flag)
            allowed = jnp.concatenate(
                [jnp.full((1, BLK), flag.astype(F32), F32) for flag in flags], axis=1
            )
            here = pl.ds(a * BLK, BLK)
            there = pl.ds(pl.multiple_of(shard * rows + a * BLK, BLK), BLK)

            def one_head(h, carry):
                lanes = pl.ds(pl.multiple_of(h * DH, DH), DH)
                scores = lax.dot_general(
                    qh[here, lanes], khat[:, lanes], (((1,), (1,)), ((), ())),
                    preferred_element_type=F32,
                )
                weights = (jnp.exp2(scores * SCORE_SCALE) * allowed).astype(BF16)
                values = vall[:, lanes]
                wide = jnp.concatenate([values, jnp.ones_like(values)], axis=1)
                both = jnp.dot(weights, wide, preferred_element_type=F32)
                out[there, lanes] = (both[:, :DH] / both[:, DH:]).astype(BF16)
                return carry

            lax.fori_loop(0, heads, one_head, 0)

    attend(me, 0)

    for h in range(1, n):
        def take(c, h=h):
            for way, shard in ((1, me - h), (0, me + h)):
                @pl.when((shard >= 0) & (shard < n))
                def _(way=way, shard=shard):
                    hop(shard, c, way).wait_recv()

                    @pl.when((me < n - 1) if way == 1 else (me > 0))
                    def _():
                        hop(shard, c, way).start()

                    project(shard, c, way)

        each(take)
        for way, shard in ((1, me - h), (0, me + h)):
            @pl.when((shard >= 0) & (shard < n))
            def _(way=way, shard=shard):
                attend(shard, way)

    for h in range(n):
        for way, shard in ((1, me - h), (0, me + h)):
            @pl.when(
                (shard >= 0) & (shard < n) & ((me < n - 1) if way == 1 else (me > 0))
            )
            def _(way=way, shard=shard):
                each(lambda c: hop(shard, c, way).wait_send())


def on_device(
    n, patches, tokens, mod_scale, mod_shift, q_weight, q_gain, stale_keys, stale_values,
    kv_lists, block_mask
):
    rows, width = tokens.shape
    cols = q_weight.shape[1]
    local = stale_keys.shape[0]
    slots = kv_lists.shape[2]
    got = (patches - 1) * slots
    keys = local + got * BLK
    vmem = pl.BlockSpec(memory_space=pltpu.VMEM)
    smem = pl.BlockSpec(memory_space=pltpu.SMEM)
    hbm = pl.BlockSpec(memory_space=pl.ANY)
    dma = pltpu.SemaphoreType.DMA
    return pl.pallas_call(
        functools.partial(body, n, patches, slots),
        out_shape=jax.ShapeDtypeStruct((local, cols), BF16),
        in_specs=[vmem, vmem, vmem, hbm, vmem, hbm, hbm, smem, smem],
        out_specs=vmem,
        scratch_shapes=[
            pltpu.VMEM((n, CHUNKS, rows, width // CHUNKS), BF16),
            pltpu.VMEM((width, cols), BF16),
            pltpu.VMEM((2, rows, cols), F32),
            pltpu.VMEM((rows, cols), BF16),
            pltpu.VMEM((keys, cols), BF16),
            pltpu.VMEM((keys, cols), BF16),
            pltpu.VMEM((keys, cols), BF16),
            pltpu.VMEM((got, 2, BLK, cols), BF16),
            dma,
            dma((2,)),
            dma((2, n, CHUNKS)),
            dma((n, CHUNKS)),
            dma((got, 2)),
            dma((got, 2)),
        ],
        compiler_params=pltpu.CompilerParams(
            collective_id=0, has_side_effects=True, vmem_limit_bytes=56 * 1024 * 1024
        ),
    )(
        tokens, mod_scale[None], mod_shift[None], q_weight, q_gain[None], stale_keys,
        stale_values, kv_lists, block_mask,
    )


def solution(mesh):
    placed = (
        P(("grp", "patch", "wring"), None),
        P(),
        P(),
        P(None, "wring"),
        P("wring"),
        P(("grp", "patch"), "wring"),
        P(("grp", "patch"), "wring"),
        P("grp", None, None),
        P("grp", None),
    )
    return jax.shard_map(
        functools.partial(on_device, mesh.shape["wring"], mesh.shape["patch"]),
        mesh=mesh,
        in_specs=placed,
        out_specs=P(("grp", "patch"), "wring"),
        check_vma=False,
    )
```

time: 179 us -> 119 us (0.66)
  Pallas kernels: 0 us -> 114 us
  waiting for transfers between devices: 92.7 us -> 0 us
  matrix products: 34.6 us -> 0 us
  between operations: 13.7 us -> 0.01 us
  local copies, waits for them, and re-layouts: 17.2 us -> 4.72 us
  other arithmetic: 11.6 us -> 0 us
  starting transfers between devices: 8.86 us -> 0 us
    pallas_call x0 -> x1, Pallas kernels: none -> 114 us  [on_device(): pl.pallas_call(functools.partial(body, n, patches, slots), out_shape=jax....]
    all_gather x1 -> x0, waiting for transfers between devices: 82.2 us -> none  [on_device(): lax.all_gather(normed, 'wring', axis=0, tiled=True)]
    dot_general x14 -> x0, matrix products: 34.6 us -> none  [the longest x6 12.7 us: on_device(): jnp.einsum('qd,kd->qk', query_head, head_keys, preferred_element_type=jnp...]
    all_to_all x2 -> x0, waiting for transfers between devices: 10.5 us -> none  [the longest x1 10.5 us: on_device(): lax.all_to_all(send_keys, 'patch', split_axis=0, concat_axis=0, tiled=True)]
    mul x7 -> x0, local copies, waits for them, and re-layouts: 10.1 us -> none  [the longest x5 8.04 us: rms_rows(): values * lax.rsqrt(jnp.mean(values * values, axis=-1, keepdims=True) + 1e...]
    all_to_all x2 -> x0, starting transfers between devices: 8.86 us -> none  [the longest x1 4.47 us: on_device(): lax.all_to_all(send_keys, 'patch', split_axis=0, concat_axis=0, tiled=True)]
    convert_element_type x5 -> x0, other arithmetic: 5.9 us -> none  [the longest x2 2.75 us: on_device(): k_hat = rms_rows(stale_keys.astype(jnp.float32).reshape(patch_rows, heads...]
    gather x2 -> x0, local copies, waits for them, and re-layouts: 3.65 us -> none  [the longest x1 1.85 us: on_device(): stale_values.reshape(blocks_here, BLK, columns)[chosen]]
  transfers between devices with their start and end apart: 3 -> 0, of which waited for: 2 -> 0; matrix products, arithmetic and copies ran while one was open for 26% -> 0% of each run, Pallas kernels for 0% -> 0%
where the time goes in v1:
time: 119 us
  Pallas kernels  114 us (96%)
  local copies, waits for them, and re-layouts  4.72 us (4%)
    pallas_call x1, Pallas kernels, on_device(): pl.pallas_call(functools.partial(body, n, patches, slots), out_shape=jax....  114 us
    unnamed x2, local copies, waits for them, and re-layouts  3.44 us

profile of v1, /device:TPU:0, one launch (start us, length us, event | category | flops | bytes accessed | tf_op | source)
XLA Modules:
  0.0 118.8 jit_solution(9709042607843975767)
XLA Ops:
  0.0 1.3 %broadcast_in_dim.11.gain = f32[1,768]{1,0:T(1,128)} reshape(f32[768]{0:T(1024)} %param.13) | data formatting | bytes 6144 | tf_op jit(solution)/shard_map/broadcast_in_dim | solution.py:268
  1.3 1.4 %copy.10.lists = s32[4,4,1]{2,1,0:T(4,128)} copy(s32[4,4,1]{1,2,0:T(1,128)} %param.16) | data formatting | bytes 128 | tf_op args[7]
  2.7 114.0 %shard_map.91 = bf16[512,768]{1,0:T(8,128)(2,1)} custom-call(bf16[128,6144]{1,0:T(8,128)(2,1)} %tok.1, f32[1,6144]{1,0:T(1,128)} %bitcast.2, f32[1,6144]{1,0:T(1,128)} %bitcast.3, bf16[6144,768]{1,0:T(8,128)(2,1)} %w_hbm.1, f32[1,768]{1,0:T(1,128)} %broadcast_in_dim.11.gain, bf16[512,768]{1,0:T(8,128)(2,1)} %k_hbm.1, bf16[512,768]{1,0:T(8,128)(2,1)} %v_hbm.1, ...), custom_call_target="tpu_custom_call" | custom-call | tf_op jit(solution)/shard_map/pallas_call | solution.py:243
  116.7 2.1 %copy.12 = bf16[512,768]{1,0:T(8,128)(2,1)} copy(bf16[512,768]{1,0:T(8,128)(2,1)} %shard_map.91) | data formatting | bytes 1572864

commit v2 on v1

--- a/solution.py
+++ b/solution.py
@@ -226,9 +226,317 @@
                 each(lambda c: hop(shard, c, way).wait_send())
 
 
+def body_assisted(
+    patches, slots,
+    tok, scale, shift, w_hbm, gain, k_hbm, v_hbm, lists, mask, out,
+    held, w, w2, acc, qh, qout, qin, kraw, vall, khat, sendkv,
+    w_sem, kv_sem, send_sem, recv_sem, ws_sem, wr_sem, qs_sem, qr_sem, kvs_sem, kvr_sem,
+):
+    me = lax.axis_index("wring")
+    mp = lax.axis_index("patch")
+    mg = lax.axis_index("grp")
+    inner = (me == 1) | (me == 2)
+    end = (me == 0) | (me == 3)
+    partner = me + 1 - 2 * lax.rem(me, 2)
+    cross = 3 - me
+    far = 3 - partner
+    core = lax.rem(mp, 2)
+    side = mp // 2
+    rows = tok.shape[0]
+    width = tok.shape[1]
+    kc = width // CHUNKS
+    piece = kc // 8
+    heads = gain.shape[1] // DH
+    local = k_hbm.shape[0]
+    bp = local // BLK
+
+    w_copy = pltpu.make_async_copy(w_hbm, w, w_sem)
+    w_copy.start()
+    k_copy = pltpu.make_async_copy(k_hbm, kraw.at[pl.ds(0, local)], kv_sem.at[0])
+    v_copy = pltpu.make_async_copy(v_hbm, vall.at[pl.ds(0, local)], kv_sem.at[1])
+    k_copy.start()
+    v_copy.start()
+
+    barrier = pltpu.get_barrier_semaphore()
+    pl.semaphore_signal(barrier, inc=1, device_id={"wring": partner})
+
+    @pl.when(inner)
+    def _():
+        pl.semaphore_signal(barrier, inc=1, device_id={"wring": cross})
+
+    pl.semaphore_signal(barrier, inc=1, device_id={"grp": 1 - mg})
+    for o in range(1, patches):
+        pl.semaphore_signal(barrier, inc=1, device_id={"patch": lax.rem(mp + o, patches)})
+    pl.semaphore_wait(barrier, jnp.where(inner, 1, 0) + 1 + patches)
+
+    def each(fn, count=CHUNKS):
+        def one(c, carry):
+            fn(c)
+            return carry
+
+        lax.fori_loop(0, count, one, 0)
+
+    def spread(stage, c):
+        odd = lax.rem(c, 2)
+        even = 1 - odd
+        first = core * 4
+        count = 1
+        where = {"wring": partner}
+        if stage in (0, 1):
+            first = first + even * (side * 2 + mg) + odd * (mg * 2 + side)
+        elif stage == 2:
+            first = first + even * (side * 2) + odd * (mg * 2)
+            count = 2
+        else:
+            count = 4
+        use_grp = even if stage == 1 else odd
+        if stage in (1, 2):
+            where = {
+                "grp": mg + use_grp * (1 - 2 * mg),
+                "patch": mp + (1 - use_grp) * (2 - 4 * side),
+            }
+        elif stage == 3:
+            where = {"patch": mp + 1 - 2 * core}
+        at = pl.ds(pl.multiple_of(c * kc + first * piece, piece), count * piece)
+        return pltpu.make_async_remote_copy(
+            src_ref=(w_hbm if stage == 0 else w2).at[at],
+            dst_ref=w2.at[at],
+            send_sem=ws_sem.at[stage, c],
+            recv_sem=wr_sem.at[stage, c],
+            device_id=where,
+        )
+
+    @pl.when(end)
+    def _():
+        each(lambda c: spread(0, c).start())
+
+    step = 16
+
+    def norm_rows(i, carry):
+        at = pl.ds(pl.multiple_of(i * step, step), step)
+        x = tok[at, :].astype(F32)
+        centred = x - jnp.mean(x, axis=-1, keepdims=True)
+        spread_of = jnp.mean(centred * centred, axis=-1, keepdims=True)
+        y = centred * lax.rsqrt(spread_of + 1e-06) * (1.0 + scale[...]) + shift[...]
+        y = y.astype(BF16)
+        for c in range(CHUNKS):
+            held[me, c, at, :] = y[:, c * kc : (c + 1) * kc]
+        return carry
+
+    lax.fori_loop(0, rows // step, norm_rows, 0)
+
+    def hop(shard, c, target):
+        return pltpu.make_async_remote_copy(
+            src_ref=held.at[shard, c],
+            dst_ref=held.at[shard, c],
+            send_sem=send_sem.at[shard, c],
+            recv_sem=recv_sem.at[shard, c],
+            device_id={"wring": target},
+        )
+
+    onward = jnp.where(inner, cross, partner)
+    each(lambda c: hop(me, c, onward).start())
+
+    k_copy.wait()
+    v_copy.wait()
+
+    def kv_copy(o, j, which):
+        slot = (o - 1) * slots + j
+        return pltpu.make_async_remote_copy(
+            src_ref=sendkv.at[slot, which],
+            dst_ref=(kraw, vall)[which].at[pl.ds(local + slot * BLK, BLK)],
+            send_sem=kvs_sem.at[slot, which],
+            recv_sem=kvr_sem.at[slot, which],
+            device_id={"patch": lax.rem(mp + o, patches)},
+        )
+
+    pairs = [(o, j) for o in range(1, patches) for j in range(slots)]
+    for o, j in pairs:
+        slot = (o - 1) * slots + j
+        picked = jnp.maximum(lists[lax.rem(mp + o, patches), mp, j], 0)
+        for which, blocks in enumerate((kraw, vall)):
+            chosen = jnp.zeros((BLK, sendkv.shape[3]), F32)
+            for b in range(bp):
+                chosen = chosen + blocks[b * BLK : (b + 1) * BLK, :].astype(F32) * (
+                    jnp.where(picked == b, 1, 0).astype(F32)
+                )
+            sendkv[slot, which] = chosen.astype(BF16)
+        kv_copy(o, j, 0).start()
+        kv_copy(o, j, 1).start()
+
+    w_copy.wait()
+
+    def add(slot, c, part):
+        @pl.when(c == 0)
+        def _():
+            acc[slot] = part
+
+        @pl.when(c > 0)
+        def _():
+            acc[slot] = acc[slot] + part
+
+    def project(shard, c, weight, slot):
+        at = pl.ds(pl.multiple_of(c * kc, kc), kc)
+        add(slot, c, jnp.dot(held[shard, c], weight[at, :], preferred_element_type=F32))
+
+    def project_two(one, two, c, weight, slot):
+        at = pl.ds(pl.multiple_of(c * kc, kc), kc)
+        both = jnp.concatenate([held[one, c], held[two, c]], axis=0)
+        part = jnp.dot(both, weight[at, :], preferred_element_type=F32)
+        add(slot, c, part[:rows])
+        add(slot + 1, c, part[rows:])
+
+    def finish_keys():
+        for o, j in pairs:
+            for which in range(2):
+                kv_copy(o, j, which).wait_recv()
+                kv_copy(o, j, which).wait_send()
+
+        def norm_keys(i, carry):
+            at = pl.ds(pl.multiple_of(i * BLK, BLK), BLK)
+            for h in range(heads):
+                lanes = slice(h * DH, (h + 1) * DH)
+                khat[at, lanes] = rms_rows(kraw[at, lanes].astype(F32)).astype(BF16)
+            return carry
+
+        lax.fori_loop(0, khat.shape[0] // BLK, norm_keys, 0)
+
+    def norm_queries(read, slot):
+        for h in range(heads):
+            lanes = slice(h * DH, (h + 1) * DH)
+            q = read(lanes).astype(BF16).astype(F32)
+            qh[slot, :, lanes] = (rms_rows(q) * gain[:, lanes]).astype(BF16)
+
+    def attend_head(shard, slot, h):
+        row = mp * bp + shard
+        flags = [mask[row, mp * bp + b] for b in range(bp)]
+        for o, j in pairs:
+            owner = lax.rem(mp + patches - o, patches)
+            listed = lists[mp, owner, j]
+            flag = 0
+            for b in range(bp):
+                flag = flag + jnp.where(listed == b, mask[row, owner * bp + b], 0)
+            flags.append(flag)
+        allowed = jnp.concatenate(
+            [jnp.full((1, BLK), flag.astype(F32), F32) for flag in flags], axis=1
+        )
+        lanes = pl.ds(pl.multiple_of(h * DH, DH), DH)
+        scores = lax.dot_general(
+            qh[slot, :, lanes], khat[:, lanes], (((1,), (1,)), ((), ())),
+            preferred_element_type=F32,
+        )
+        weights = (jnp.exp2(scores * SCORE_SCALE) * allowed).astype(BF16)
+        values = vall[:, lanes]
+        wide = jnp.concatenate([values, jnp.ones_like(values)], axis=1)
+        both = jnp.dot(weights, wide, preferred_element_type=F32)
+        there = pl.ds(pl.multiple_of(shard * rows, rows), rows)
+        out[there, lanes] = (both[:, :DH] / both[:, DH:]).astype(BF16)
+
+    def give(shard):
+        return pltpu.make_async_remote_copy(
+            src_ref=qout.at[shard],
+            dst_ref=qin.at[shard],
+            send_sem=qs_sem.at[shard],
+            recv_sem=qr_sem.at[shard],
+            device_id={"wring": partner},
+        )
+
+    @pl.when(inner)
+    def _():
+        def advance(c):
+            @pl.when(c < CHUNKS)
+            def _():
+                spread(0, c).wait_recv()
+                spread(1, c).start()
+
+            @pl.when((c >= 1) & (c <= CHUNKS))
+            def _():
+                spread(1, c - 1).wait_recv()
+                spread(2, c - 1).start()
+
+            @pl.when((c >= 2) & (c <= CHUNKS + 1))
+            def _():
+                spread(2, c - 2).wait_recv()
+                spread(3, c - 2).start()
+
+        def early(c):
+            advance(c)
+            hop(cross, c, cross).wait_recv()
+            project_two(me, cross, c, w, 0)
+
+        each(early)
+        finish_keys()
+        norm_queries(lambda lanes: acc[0, :, lanes], 0)
+        norm_queries(lambda lanes: acc[1, :, lanes], 1)
+
+        def middle(c):
+            hop(partner, c, cross).wait_recv()
+            hop(partner, c, cross).start()
+
+            @pl.when(c < 2)
+            def _():
+                advance(c + CHUNKS)
+
+            project(partner, c, w, 2)
+            spread(3, c).wait_recv()
+            project_two(me, cross, c, w2, 3)
+
+            @pl.when(c < heads)
+            def _():
+                attend_head(me, 0, c)
+                attend_head(cross, 1, c)
+
+        each(middle)
+        qout[me] = acc[3].astype(BF16)
+        give(me).start()
+        qout[cross] = acc[4].astype(BF16)
+        give(cross).start()
+        norm_queries(lambda lanes: acc[2, :, lanes], 0)
+        each(lambda h: attend_head(partner, 0, h), heads)
+
+        def late(c):
+            hop(far, c, cross).wait_recv()
+            project(far, c, w2, 5)
+            project(far, c, w, 2)
+
+        each(late)
+        qout[far] = acc[5].astype(BF16)
+        give(far).start()
+        norm_queries(lambda lanes: acc[2, :, lanes], 0)
+        each(lambda h: attend_head(far, 0, h), heads)
+
+        def settle(c):
+            hop(me, c, cross).wait_send()
+            hop(partner, c, cross).wait_send()
+            for stage in (1, 2, 3):
+                spread(stage, c).wait_send()
+
+        each(settle)
+        for shard in (me, cross, far):
+            give(shard).wait_send()
+
+    @pl.when(end)
+    def _():
+        each(lambda c: project(me, c, w, 0))
+        finish_keys()
+        norm_queries(lambda lanes: acc[0, :, lanes], 0)
+        each(lambda h: attend_head(me, 0, h), heads)
+
+        def settle(c):
+            hop(me, c, partner).wait_send()
+            spread(0, c).wait_send()
+
+        each(settle)
+
+        for shard in (partner, far, cross):
+            give(shard).wait_recv()
+            norm_queries(lambda lanes: qin[shard, :, lanes], 0)
+            each(lambda h: attend_head(shard, 0, h), heads)
+
+
 def on_device(
-    n, patches, tokens, mod_scale, mod_shift, q_weight, q_gain, stale_keys, stale_values,
-    kv_lists, block_mask
+    n, patches, groups, tokens, mod_scale, mod_shift, q_weight, q_gain, stale_keys,
+    stale_values, kv_lists, block_mask
 ):
     rows, width = tokens.shape
     cols = q_weight.shape[1]
@@ -240,27 +548,47 @@
     smem = pl.BlockSpec(memory_space=pltpu.SMEM)
     hbm = pl.BlockSpec(memory_space=pl.ANY)
     dma = pltpu.SemaphoreType.DMA
+    assisted = (
+        (n, patches, groups) == (4, 4, 2)
+        and rows == BLK
+        and cols // DH <= CHUNKS
+        and width % (CHUNKS * 8 * 16) == 0
+    )
+    held = pltpu.VMEM((n, CHUNKS, rows, width // CHUNKS), BF16)
+    w = pltpu.VMEM((width, cols), BF16)
+    by_key = [pltpu.VMEM((keys, cols), BF16)] * 3 + [pltpu.VMEM((got, 2, BLK, cols), BF16)]
+    if assisted:
+        kernel = functools.partial(body_assisted, patches, slots)
+        scratch = [
+            held, w, w,
+            pltpu.VMEM((6, rows, cols), F32),
+            pltpu.VMEM((2, rows, cols), BF16),
+            pltpu.VMEM((n, rows, cols), BF16),
+            pltpu.VMEM((n, rows, cols), BF16),
+            *by_key,
+            dma, dma((2,)),
+            dma((n, CHUNKS)), dma((n, CHUNKS)),
+            dma((4, CHUNKS)), dma((4, CHUNKS)),
+            dma((n,)), dma((n,)),
+            dma((got, 2)), dma((got, 2)),
+        ]
+    else:
+        kernel = functools.partial(body, n, patches, slots)
+        scratch = [
+            held, w,
+            pltpu.VMEM((2, rows, cols), F32),
+            pltpu.VMEM((rows, cols), BF16),
+            *by_key,
+            dma, dma((2,)),
+            dma((2, n, CHUNKS)), dma((n, CHUNKS)),
+            dma((got, 2)), dma((got, 2)),
+        ]
     return pl.pallas_call(
-        functools.partial(body, n, patches, slots),
+        kernel,
         out_shape=jax.ShapeDtypeStruct((local, cols), BF16),
         in_specs=[vmem, vmem, vmem, hbm, vmem, hbm, hbm, smem, smem],
         out_specs=vmem,
-        scratch_shapes=[
-            pltpu.VMEM((n, CHUNKS, rows, width // CHUNKS), BF16),
-            pltpu.VMEM((width, cols), BF16),
-            pltpu.VMEM((2, rows, cols), F32),
-            pltpu.VMEM((rows, cols), BF16),
-            pltpu.VMEM((keys, cols), BF16),
-            pltpu.VMEM((keys, cols), BF16),
-            pltpu.VMEM((keys, cols), BF16),
-            pltpu.VMEM((got, 2, BLK, cols), BF16),
-            dma,
-            dma((2,)),
-            dma((2, n, CHUNKS)),
-            dma((n, CHUNKS)),
-            dma((got, 2)),
-            dma((got, 2)),
-        ],
+        scratch_shapes=scratch,
         compiler_params=pltpu.CompilerParams(
             collective_id=0, has_side_effects=True, vmem_limit_bytes=56 * 1024 * 1024
         ),
@@ -283,7 +611,7 @@
         P("grp", None),
     )
     return jax.shard_map(
-        functools.partial(on_device, mesh.shape["wring"], mesh.shape["patch"]),
+        functools.partial(on_device, mesh.shape["wring"], mesh.shape["patch"], mesh.shape["grp"]),
         mesh=mesh,
         in_specs=placed,
         out_specs=P(("grp", "patch"), "wring"),

time: 119 us -> 113 us (0.950)
  Pallas kernels: 114 us -> 108 us
    pallas_call x1, Pallas kernels: 114 us -> 108 us  [on_device(): pl.pallas_call(kernel, out_shape=jax.ShapeDtypeStruct((local, cols), BF16...]
where the time goes in v2:
time: 113 us
  Pallas kernels  108 us (96%)
  local copies, waits for them, and re-layouts  4.72 us (4%)
    pallas_call x1, Pallas kernels, on_device(): pl.pallas_call(kernel, out_shape=jax.ShapeDtypeStruct((local, cols), BF16...  108 us
    unnamed x2, local copies, waits for them, and re-layouts  3.44 us

profile of v2, /device:TPU:0, one launch (start us, length us, event | category | flops | bytes accessed | tf_op | source)
XLA Modules:
  0.0 112.9 jit_solution(12392341028352665161)
XLA Ops:
  0.0 1.3 %broadcast_in_dim.11.gain = f32[1,768]{1,0:T(1,128)} reshape(f32[768]{0:T(1024)} %param.13) | data formatting | bytes 6144 | tf_op jit(solution)/shard_map/broadcast_in_dim | solution.py:596
  1.3 1.4 %copy.10.lists = s32[4,4,1]{2,1,0:T(4,128)} copy(s32[4,4,1]{1,2,0:T(1,128)} %param.16) | data formatting | bytes 128 | tf_op args[7]
  2.7 108.2 %shard_map.91 = bf16[512,768]{1,0:T(8,128)(2,1)} custom-call(bf16[128,6144]{1,0:T(8,128)(2,1)} %tok.1, f32[1,6144]{1,0:T(1,128)} %bitcast.2, f32[1,6144]{1,0:T(1,128)} %bitcast.3, bf16[6144,768]{1,0:T(8,128)(2,1)} %w_hbm.1, f32[1,768]{1,0:T(1,128)} %broadcast_in_dim.11.gain, bf16[512,768]{1,0:T(8,128)(2,1)} %k_hbm.1, bf16[512,768]{1,0:T(8,128)(2,1)} %v_hbm.1, ...), custom_call_target="tpu_custom_call" | custom-call | tf_op jit(solution)/shard_map/pallas_call | solution.py:586
  110.8 2.1 %copy.12 = bf16[512,768]{1,0:T(8,128)(2,1)} copy(bf16[512,768]{1,0:T(8,128)(2,1)} %shard_map.91) | data formatting | bytes 1572864

commit v3 on v2

--- a/solution.py
+++ b/solution.py
@@ -11,6 +11,7 @@
 DH = 128
 BLK = 128
 CHUNKS = 8
+AHEAD = 3
 F32 = jnp.float32
 BF16 = jnp.bfloat16
 SCORE_SCALE = math.log2(math.e) / math.sqrt(DH)
@@ -31,7 +32,7 @@
     rows = tok.shape[0]
     width = tok.shape[1]
     kc = width // CHUNKS
-    heads = gain.shape[1] // DH
+    heads = gain.shape[0] // DH
     local = k_hbm.shape[0]
     bp = local // BLK
 
@@ -62,7 +63,7 @@
         x = tok[at, :].astype(F32)
         centred = x - jnp.mean(x, axis=-1, keepdims=True)
         spread = jnp.mean(centred * centred, axis=-1, keepdims=True)
-        y = centred * lax.rsqrt(spread + 1e-06) * (1.0 + scale[...]) + shift[...]
+        y = centred * lax.rsqrt(spread + 1e-06) * (1.0 + scale[...][None]) + shift[...][None]
         y = y.astype(BF16)
         for c in range(CHUNKS):
             held[me, c, at, :] = y[:, c * kc : (c + 1) * kc]
@@ -164,7 +165,7 @@
         for h in range(heads):
             lanes = slice(h * DH, (h + 1) * DH)
             q = acc[way, :, lanes].astype(BF16).astype(F32)
-            qh[:, lanes] = (rms_rows(q) * gain[:, lanes]).astype(BF16)
+            qh[:, lanes] = (rms_rows(q) * gain[lanes][None]).astype(BF16)
         for a in range(rows // BLK):
             row = mp * bp + shard * (rows // BLK) + a
             flags = [mask[row, mp * bp + b] for b in range(bp)]
@@ -246,7 +247,7 @@
     width = tok.shape[1]
     kc = width // CHUNKS
     piece = kc // 8
-    heads = gain.shape[1] // DH
+    heads = gain.shape[0] // DH
     local = k_hbm.shape[0]
     bp = local // BLK
 
@@ -277,7 +278,7 @@
         lax.fori_loop(0, count, one, 0)
 
     def spread(stage, c):
-        odd = lax.rem(c, 2)
+        odd = jnp.where(lax.rem(c, 4) == 3, 1, 0)
         even = 1 - odd
         first = core * 4
         count = 1
@@ -317,7 +318,7 @@
         x = tok[at, :].astype(F32)
         centred = x - jnp.mean(x, axis=-1, keepdims=True)
         spread_of = jnp.mean(centred * centred, axis=-1, keepdims=True)
-        y = centred * lax.rsqrt(spread_of + 1e-06) * (1.0 + scale[...]) + shift[...]
+        y = centred * lax.rsqrt(spread_of + 1e-06) * (1.0 + scale[...][None]) + shift[...][None]
         y = y.astype(BF16)
         for c in range(CHUNKS):
             held[me, c, at, :] = y[:, c * kc : (c + 1) * kc]
@@ -334,8 +335,10 @@
             device_id={"wring": target},
         )
 
-    onward = jnp.where(inner, cross, partner)
-    each(lambda c: hop(me, c, onward).start())
+    @pl.when(inner)
+    def _():
+        for c in range(AHEAD):
+            hop(me, c, cross).start()
 
     k_copy.wait()
     v_copy.wait()
@@ -386,26 +389,23 @@
         add(slot, c, part[:rows])
         add(slot + 1, c, part[rows:])
 
-    def finish_keys():
+    def wait_keys():
         for o, j in pairs:
             for which in range(2):
                 kv_copy(o, j, which).wait_recv()
                 kv_copy(o, j, which).wait_send()
 
-        def norm_keys(i, carry):
-            at = pl.ds(pl.multiple_of(i * BLK, BLK), BLK)
-            for h in range(heads):
-                lanes = slice(h * DH, (h + 1) * DH)
-                khat[at, lanes] = rms_rows(kraw[at, lanes].astype(F32)).astype(BF16)
-            return carry
-
-        lax.fori_loop(0, khat.shape[0] // BLK, norm_keys, 0)
+    def norm_keys(i):
+        at = pl.ds(pl.multiple_of(i * BLK, BLK), BLK)
+        for h in range(heads):
+            lanes = slice(h * DH, (h + 1) * DH)
+            khat[at, lanes] = rms_rows(kraw[at, lanes].astype(F32)).astype(BF16)
 
     def norm_queries(read, slot):
         for h in range(heads):
             lanes = slice(h * DH, (h + 1) * DH)
             q = read(lanes).astype(BF16).astype(F32)
-            qh[slot, :, lanes] = (rms_rows(q) * gain[:, lanes]).astype(BF16)
+            qh[slot, :, lanes] = (rms_rows(q) * gain[lanes][None]).astype(BF16)
 
     def attend_head(shard, slot, h):
         row = mp * bp + shard
@@ -449,44 +449,64 @@
                 spread(0, c).wait_recv()
                 spread(1, c).start()
 
-            @pl.when((c >= 1) & (c <= CHUNKS))
-            def _():
-                spread(1, c - 1).wait_recv()
-                spread(2, c - 1).start()
-
-            @pl.when((c >= 2) & (c <= CHUNKS + 1))
-            def _():
-                spread(2, c - 2).wait_recv()
-                spread(3, c - 2).start()
+            @pl.when((c >= 2) & (c < CHUNKS + 2))
+            def _():
+                spread(1, c - 2).wait_recv()
+                spread(2, c - 2).start()
+
+            @pl.when((c >= 4) & (c < CHUNKS + 4))
+            def _():
+                spread(2, c - 4).wait_recv()
+                spread(3, c - 4).start()
 
         def early(c):
+            @pl.when(c + AHEAD < CHUNKS)
+            def _():
+                hop(me, c + AHEAD, cross).start()
+
             advance(c)
             hop(cross, c, cross).wait_recv()
             project_two(me, cross, c, w, 0)
 
+            @pl.when(c < bp)
+            def _():
+                norm_keys(c)
+
+            @pl.when(c == bp + 1)
+            def _():
+                wait_keys()
+
+            @pl.when(c > bp)
+            def _():
+                norm_keys(c - 1)
+
         each(early)
-        finish_keys()
-        norm_queries(lambda lanes: acc[0, :, lanes], 0)
-        norm_queries(lambda lanes: acc[1, :, lanes], 1)
 
         def middle(c):
             hop(partner, c, cross).wait_recv()
             hop(partner, c, cross).start()
 
-            @pl.when(c < 2)
-            def _():
-                advance(c + CHUNKS)
+            @pl.when(c == 0)
+            def _():
+                norm_queries(lambda lanes: acc[0, :, lanes], 0)
+                norm_queries(lambda lanes: acc[1, :, lanes], 1)
 
             project(partner, c, w, 2)
+
+            @pl.when(c < heads)
+            def _():
+                attend_head(me, 0, c)
+                attend_head(cross, 1, c)
+
+        each(middle)
+        for c in range(4):
+            advance(jnp.int32(c + CHUNKS))
+
+        def borrowed(c):
             spread(3, c).wait_recv()
             project_two(me, cross, c, w2, 3)
 
-            @pl.when(c < heads)
-            def _():
-                attend_head(me, 0, c)
-                attend_head(cross, 1, c)
-
-        each(middle)
+        each(borrowed)
         qout[me] = acc[3].astype(BF16)
         give(me).start()
         qout[cross] = acc[4].astype(BF16)
@@ -517,16 +537,20 @@
 
     @pl.when(end)
     def _():
+        for c in range(CHUNKS - 1):
+            spread(0, c).wait_send()
+        each(lambda c: hop(me, c, partner).start())
         each(lambda c: project(me, c, w, 0))
-        finish_keys()
+        wait_keys()
+        each(norm_keys, khat.shape[0] // BLK)
         norm_queries(lambda lanes: acc[0, :, lanes], 0)
         each(lambda h: attend_head(me, 0, h), heads)
 
         def settle(c):
             hop(me, c, partner).wait_send()
-            spread(0, c).wait_send()
 
         each(settle)
+        spread(0, CHUNKS - 1).wait_send()
 
         for shard in (partner, far, cross):
             give(shard).wait_recv()
@@ -552,6 +576,7 @@
         (n, patches, groups) == (4, 4, 2)
         and rows == BLK
         and cols // DH <= CHUNKS
+        and (local // BLK, slots, CHUNKS) == (4, 1, 8)
         and width % (CHUNKS * 8 * 16) == 0
     )
     held = pltpu.VMEM((n, CHUNKS, rows, width // CHUNKS), BF16)
@@ -593,7 +618,7 @@
             collective_id=0, has_side_effects=True, vmem_limit_bytes=56 * 1024 * 1024
         ),
     )(
-        tokens, mod_scale[None], mod_shift[None], q_weight, q_gain[None], stale_keys,
+        tokens, mod_scale, mod_shift, q_weight, q_gain, stale_keys,
         stale_values, kv_lists, block_mask,
     )
 

time: 113 us -> 102 us (0.903)
  Pallas kernels: 108 us -> 98 us
  local copies, waits for them, and re-layouts: 4.72 us -> 3.44 us
    pallas_call x1, Pallas kernels: 108 us -> 98 us  [on_device(): pl.pallas_call(kernel, out_shape=jax.ShapeDtypeStruct((local, cols), BF16...]
    broadcast_in_dim x1 -> x0, local copies, waits for them, and re-layouts: 1.28 us -> none  [on_device(): q_gain[None]]
where the time goes in v3:
time: 102 us; the launch traced here: 101 us
  Pallas kernels  98 us (96%)
  local copies, waits for them, and re-layouts  3.44 us (3%)
    pallas_call x1, Pallas kernels, on_device(): pl.pallas_call(kernel, out_shape=jax.ShapeDtypeStruct((local, cols), BF16...  98 us
    unnamed x2, local copies, waits for them, and re-layouts  3.44 us

profile of v3, /device:TPU:0, one launch (start us, length us, event | category | flops | bytes accessed | tf_op | source)
XLA Modules:
  0.0 101.4 jit_solution(4551385341556602716)
XLA Ops:
  0.0 1.4 %copy.10.lists = s32[4,4,1]{2,1,0:T(4,128)} copy(s32[4,4,1]{1,2,0:T(1,128)} %param.16) | data formatting | bytes 128 | tf_op args[7]
  1.4 98.0 %shard_map.91 = bf16[512,768]{1,0:T(8,128)(2,1)} custom-call(bf16[128,6144]{1,0:T(8,128)(2,1)} %tok.1, f32[6144]{0:T(1024)} %scale.1, f32[6144]{0:T(1024)} %shift.1, bf16[6144,768]{1,0:T(8,128)(2,1)} %w_hbm.1, f32[768]{0:T(1024)} %gain.1, bf16[512,768]{1,0:T(8,128)(2,1)} %k_hbm.1, bf16[512,768]{1,0:T(8,128)(2,1)} %v_hbm.1, s32[4,4,1]{2,1,0:T(4,128)} %copy.10.lists, ...), custom_call_target="tpu_custom_call" | custom-call | tf_op jit(solution)/shard_map/pallas_call | solution.py:611
  99.4 2.1 %copy.12 = bf16[512,768]{1,0:T(8,128)(2,1)} copy(bf16[512,768]{1,0:T(8,128)(2,1)} %shard_map.91) | data formatting | bytes 1572864

commit v4 on v3

--- a/solution.py
+++ b/solution.py
@@ -502,6 +502,9 @@
         for c in range(4):
             advance(jnp.int32(c + CHUNKS))
 
+        norm_queries(lambda lanes: acc[2, :, lanes], 0)
+        each(lambda h: attend_head(partner, 0, h), heads)
+
         def borrowed(c):
             spread(3, c).wait_recv()
             project_two(me, cross, c, w2, 3)
@@ -511,17 +514,15 @@
         give(me).start()
         qout[cross] = acc[4].astype(BF16)
         give(cross).start()
-        norm_queries(lambda lanes: acc[2, :, lanes], 0)
-        each(lambda h: attend_head(partner, 0, h), heads)
 
         def late(c):
             hop(far, c, cross).wait_recv()
             project(far, c, w2, 5)
-            project(far, c, w, 2)
 
         each(late)
         qout[far] = acc[5].astype(BF16)
         give(far).start()
+        each(lambda c: project(far, c, w, 2))
         norm_queries(lambda lanes: acc[2, :, lanes], 0)
         each(lambda h: attend_head(far, 0, h), heads)
 

time: 102 us -> 104 us (1.020)
  Pallas kernels: 98 us -> 100 us
    pallas_call x1, Pallas kernels: 98 us -> 100 us  [on_device(): pl.pallas_call(kernel, out_shape=jax.ShapeDtypeStruct((local, cols), BF16...]
where the time goes in v4:
time: 104 us; the launch traced here: 103 us
  Pallas kernels  100 us (96%)
  local copies, waits for them, and re-layouts  3.44 us (3%)
    pallas_call x1, Pallas kernels, on_device(): pl.pallas_call(kernel, out_shape=jax.ShapeDtypeStruct((local, cols), BF16...  100 us
    unnamed x2, local copies, waits for them, and re-layouts  3.44 us

profile of v4, /device:TPU:0, one launch (start us, length us, event | category | flops | bytes accessed | tf_op | source)
XLA Modules:
  0.0 103.4 jit_solution(8085176316455606641)
XLA Ops:
  0.0 1.4 %copy.10.lists = s32[4,4,1]{2,1,0:T(4,128)} copy(s32[4,4,1]{1,2,0:T(1,128)} %param.16) | data formatting | bytes 128 | tf_op args[7]
  1.4 100.0 %shard_map.91 = bf16[512,768]{1,0:T(8,128)(2,1)} custom-call(bf16[128,6144]{1,0:T(8,128)(2,1)} %tok.1, f32[6144]{0:T(1024)} %scale.1, f32[6144]{0:T(1024)} %shift.1, bf16[6144,768]{1,0:T(8,128)(2,1)} %w_hbm.1, f32[768]{0:T(1024)} %gain.1, bf16[512,768]{1,0:T(8,128)(2,1)} %k_hbm.1, bf16[512,768]{1,0:T(8,128)(2,1)} %v_hbm.1, s32[4,4,1]{2,1,0:T(4,128)} %copy.10.lists, ...), custom_call_target="tpu_custom_call" | custom-call | tf_op jit(solution)/shard_map/pallas_call | solution.py:612
  101.4 2.1 %copy.12 = bf16[512,768]{1,0:T(8,128)(2,1)} copy(bf16[512,768]{1,0:T(8,128)(2,1)} %shard_map.91) | data formatting | bytes 1572864
